TPU v7x, 32 devices: a whole 2x2x4 slice. The times are simulated.
32 devices in a mesh: feat: 2 (over x), samp: 16 (over z, y, core).
Axes of the slice: x: 2, y: 2, z: 4, core: 2. Of those that a mesh axis runs over, the one named last changes fastest.
Arguments:
- samples: bfloat16 [6144, 32768], P('samp', 'feat'), may hold values from -6 to 6
- factor: float32 [32768, 128], P(('feat', 'samp')), as said below
Outputs:
- factor_out: float32 [32768, 128], P(('feat', 'samp'))
- gradient: float32 [32768, 128], P(('feat', 'samp'))
Inputs may be any that keep to these rules, and one draw needn't show every extreme that they name: `factor`: each entry's magnitude is below 40 * 32768 ** -0.4.
All inputs are finite; a program needn't handle non-finite values.
Results may differ from a plain program's by a relative error of at most 0.0074.
Values may be sent and summed in bfloat16 or wider, within the bound.
A program may use at most 64 MiB of HBM per device.

v0:
```python
import jax
import jax.numpy as jnp
from jax import lax
from jax.sharding import PartitionSpec as P

ITERS = 2


step_size = 0.00025


def moment_owned(samples, square):
    return lax.psum_scatter(
        lax.dot_general(
            samples, square, (((0,), (0,)), ((), ())), preferred_element_type=jnp.float32
        ),
        "samp",
        scatter_dimension=0,
        tiled=True,
    )


def squared_rows(partial_value):
    proj = lax.psum(partial_value, "feat")
    return (proj * proj).astype(jnp.bfloat16)


def model_term(rows, gram):
    return jnp.dot(
        rows, gram * gram, precision=lax.Precision.HIGHEST, preferred_element_type=jnp.float32
    )


def self_gram(rows):
    return lax.dot_general(
        rows,
        rows,
        (((0,), (0,)), ((), ())),
        precision=lax.Precision.HIGHEST,
        preferred_element_type=jnp.float32,
    )


def project_rows(samples, a_half):
    return jnp.dot(
        samples,
        lax.all_gather(a_half, "samp", axis=0, tiled=True),
        preferred_element_type=jnp.float32,
    )


def local(samples, factor):
    total = samples.shape[0] * lax.axis_size("samp")
    inv_root = 1.0 / jnp.sqrt(jnp.float32(total))
    current = factor
    gradient = jnp.zeros_like(factor)
    for step in range(ITERS):
        a_half = current.astype(jnp.bfloat16)
        partial_value = project_rows(samples, a_half)
        square = squared_rows(partial_value)
        gram = lax.psum(self_gram(current), ("feat", "samp"))
        moment = moment_owned(samples, square)
        gradient = moment * inv_root - model_term(current, gram)
        current = current + step_size * gradient
    return (current, gradient)


def solution(mesh):
    in_specs = (P("samp", "feat"), P(("feat", "samp"), None))
    out_specs = (P(("feat", "samp"), None), P(("feat", "samp"), None))
    return jax.shard_map(local, mesh=mesh, in_specs=in_specs, out_specs=out_specs, check_vma=False)
```

profile of v0, /device:TPU:0, one launch (start us, length us, event | category | flops | bytes accessed | tf_op | source)
XLA Modules:
  0.0 656.5 jit_solution(6052529034016222327)
XLA Ops:
  7.2 0.0 copy-start
  7.2 0.0 all-gather.3.cloned.1.call-start
  7.2 1.8 convert_element_type.12
  9.0 0.0 all-gather.3.cloned.1.call-update
  9.1 0.0 all-reduce.5.cloned.1.call-start
  9.1 54.9 %all-gather.3.cloned.1.call-done = bf16[16384,128]{1,0:T(8,128)(2,1)} async-done(((bf16[1024,128]{1,0:T(8,128)(2,1)}), bf16[16384,128]{1,0:T(8,128)(2,1)}) %all-gather.3.cloned.1.call-update) | async-done | bytes 4194320 | tf_op jit(solution)/shard_map/all_gather | solution.py:47
  64.0 9.9 %fusion.6 = f32[384,128]{1,0:T(8,128)} fusion(bf16[384,16384]{1,0:T(8,128)(2,1)} %param.2, bf16[16384,128]{1,0:T(8,128)(2,1)} %all-gather.3.cloned.1.call-done), kind=kOutput, calls=%fused_computation.14 | convolution fusion | flops 1610612736 | bytes 16973824 | tf_op jit(solution)/shard_map/dot_general | solution.py:45
  73.9 0.0 all-reduce.5.cloned.1.call-update
  73.9 0.0 all-reduce.7.cloned.1.call-start
  74.0 0.0 copy-done
  74.0 1.6 fusion.7
  75.6 0.0 all-reduce.7.cloned.1.call-update
  75.6 0.0 reduce-scatter.3.cloned.1.call-start
  75.7 19.2 %all-reduce.5.cloned.1.call-done = f32[384,128]{1,0:T(8,128)} async-done(((f32[384,128]{1,0:T(8,128)}), f32[384,128]{1,0:T(8,128)}) %all-reduce.5.cloned.1.call-update) | async-done | bytes 196624 | tf_op jit(solution)/shard_map/psum | solution.py:24
  94.9 10.3 %convolution_bitcast_fusion.1 = f32[16384,128]{0,1:T(8,128)} fusion(bf16[384,16384]{1,0:T(8,128)(2,1)} %param.2, f32[384,128]{1,0:T(8,128)} %all-reduce.5.cloned.1.call-done), kind=kOutput, calls=%fused_computation.1 | convolution fusion | flops 1610711040 | bytes 21168128 | tf_op jit(solution)/shard_map/dot_general | solution.py:14
  105.2 0.0 reduce-scatter.3.cloned.1.call-update
  105.2 0.0 all-gather.5.cloned.1.call-start
  105.2 0.2 copy.4
  105.4 113.1 %all-reduce.7.cloned.1.call-done = f32[128,128]{1,0:T(8,128)} async-done(((f32[128,128]{1,0:T(8,128)}), f32[128,128]{1,0:T(8,128)}) %all-reduce.7.cloned.1.call-update) | async-done | bytes 65552 | tf_op jit(solution)/shard_map/psum | solution.py:61
  218.6 109.6 %reduce-scatter.3.cloned.1.call-done = f32[1024,128]{0,1:T(8,128)} async-done(((f32[16384,128]{0,1:T(8,128)}), f32[1024,128]{0,1:T(8,128)}) %reduce-scatter.3.cloned.1.call-update) | async-done | bytes 524304 | tf_op jit(solution)/shard_map/reduce_scatter | solution.py:13
  328.2 2.5 fusion.5
  330.7 0.0 all-gather.5.cloned.1.call-update
  330.7 0.0 all-reduce.9.cloned.1.call-start
  330.7 50.4 %all-gather.5.cloned.1.call-done = bf16[16384,128]{0,1:T(8,128)(2,1)} async-done(((bf16[1024,128]{0,1:T(8,128)(2,1)}), bf16[16384,128]{0,1:T(8,128)(2,1)}) %all-gather.5.cloned.1.call-update) | async-done | bytes 4194320 | tf_op jit(solution)/shard_map/all_gather | solution.py:47
  381.2 10.3 %convolution_bitcast_fusion.3 = f32[384,128]{0,1:T(8,128)} fusion(bf16[16384,128]{0,1:T(8,128)(2,1)} %all-gather.5.cloned.1.call-done, bf16[384,16384]{1,0:T(8,128)(2,1)} %param.2), kind=kOutput, calls=%fused_computation.7 | convolution fusion | flops 1610612736 | bytes 16973824 | tf_op jit(solution)/shard_map/dot_general | solution.py:45
  391.5 0.0 all-reduce.9.cloned.1.call-update
  391.5 0.0 all-reduce.11.cloned.1.call-start
  391.6 1.2 fusion.8
  392.8 0.0 all-reduce.11.cloned.1.call-update
  392.8 0.2 reduce-scatter.5.cloned.1.call-start
  393.1 19.4 %all-reduce.9.cloned.1.call-done = f32[384,128]{0,1:T(8,128)} async-done(((f32[384,128]{0,1:T(8,128)}), f32[384,128]{0,1:T(8,128)}) %all-reduce.9.cloned.1.call-update) | async-done | bytes 196624 | tf_op jit(solution)/shard_map/psum | solution.py:24
  412.5 10.3 %convolution_bitcast_fusion = f32[16384,128]{0,1:T(8,128)} fusion(bf16[384,16384]{1,0:T(8,128)(2,1)} %param.2, f32[384,128]{0,1:T(8,128)} %all-reduce.9.cloned.1.call-done), kind=kOutput, calls=%fused_computation | convolution fusion | flops 1610711040 | bytes 21168128 | tf_op jit(solution)/shard_map/dot_general | solution.py:14
  422.8 0.0 reduce-scatter.5.cloned.1.call-update
  422.8 113.4 %all-reduce.11.cloned.1.call-done = f32[128,128]{1,0:T(8,128)} async-done(((f32[128,128]{1,0:T(8,128)}), f32[128,128]{1,0:T(8,128)}) %all-reduce.11.cloned.1.call-update) | async-done | bytes 65552 | tf_op jit(solution)/shard_map/psum | solution.py:61
  536.2 109.8 %reduce-scatter.5.cloned.1.call-done = f32[1024,128]{0,1:T(8,128)} async-done(((f32[16384,128]{0,1:T(8,128)}), f32[1024,128]{0,1:T(8,128)}) %reduce-scatter.5.cloned.1.call-update) | async-done | bytes 524304 | tf_op jit(solution)/shard_map/reduce_scatter | solution.py:13
  645.9 1.8 multiply_add_fusion
  647.7 1.0 copy.6
  648.7 1.0 copy.7
Async XLA Ops:
  7.2 66.8 %copy-start = (f32[1024,128]{1,0:T(8,128)S(1)}, f32[1024,128]{1,0:T(8,128)}, u32[]{:S(2)}) copy-start(f32[1024,128]{1,0:T(8,128)} %param.3) | copy-start | bytes 1572868
  7.2 56.9 %all-gather.3.cloned.1.call-start = ((), (), s32[]{:S(2)}) async-start(), calls=%async_computation.2 | async-start | bytes 4456448 | tf_op jit(solution)/shard_map/all_gather | solution.py:47
  9.1 85.8 %all-reduce.5.cloned.1.call-start = ((), (), s32[]{:S(2)}) async-start(), calls=%async_computation.3 | async-start | bytes 393216 | tf_op jit(solution)/shard_map/psum | solution.py:24
  73.9 144.6 %all-reduce.7.cloned.1.call-start = ((), (), s32[]{:S(2)}) async-start(), calls=%async_computation.5 | async-start | bytes 131072 | tf_op jit(solution)/shard_map/psum | solution.py:61
  75.6 252.5 %reduce-scatter.3.cloned.1.call-start = ((), (), s32[]{:S(2)}) async-start(), calls=%async_computation.4 | async-start | bytes 8912896 | tf_op jit(solution)/shard_map/reduce_scatter | solution.py:13
  105.2 276.0 %all-gather.5.cloned.1.call-start = ((), (), s32[]{:S(2)}) async-start(), calls=%async_computation.6 | async-start | bytes 4456448 | tf_op jit(solution)/shard_map/all_gather | solution.py:47
  330.7 81.8 %all-reduce.9.cloned.1.call-start = ((), (), s32[]{:S(2)}) async-start(), calls=%async_computation.7 | async-start | bytes 393216 | tf_op jit(solution)/shard_map/psum | solution.py:24
  391.5 144.6 %all-reduce.11.cloned.1.call-start = ((), (), s32[]{:S(2)}) async-start(), calls=%async_computation.9 | async-start | bytes 131072 | tf_op jit(solution)/shard_map/psum | solution.py:61
  392.8 253.1 %reduce-scatter.5.cloned.1.call-start = ((), (), s32[]{:S(2)}) async-start(), calls=%async_computation.8 | async-start | bytes 8912896 | tf_op jit(solution)/shard_map/reduce_scatter | solution.py:13
Sparse Core Ops, SparseCore 0:
  10.7 53.2 all-gather.2
  74.0 20.7 all-reduce.4
  101.0 117.4 all-reduce.6
  222.5 105.6 reduce-scatter.2
  330.8 50.3 all-gather.4
  391.7 20.7 all-reduce.8
  418.7 117.4 all-reduce.10
  540.3 105.6 reduce-scatter.4
where the time goes:
time: 657 us
  waiting for transfers between devices  590 us (90%)
  matrix products  47.9 us (7%)
  between operations  14.2 us (2%)
    psum x2, waiting for transfers between devices, local(): gram = lax.psum(self_gram(current), ('feat', 'samp'))  226 us
    reduce_scatter x2, waiting for transfers between devices, moment_owned(): lax.psum_scatter(lax.dot_general(samples, square, (((0,), (0,)), ((), ())...  219 us
    all_gather x2, waiting for transfers between devices, project_rows(): lax.all_gather(a_half, 'samp', axis=0, tiled=True)  105 us
    psum x2, waiting for transfers between devices, squared_rows(): proj = lax.psum(partial_value, 'feat')  38.6 us
    dot_general x2, matrix products, moment_owned(): lax.dot_general(samples, square, (((0,), (0,)), ((), ())), preferred_elem...  20.6 us
    dot_general x2, matrix products, project_rows(): jnp.dot(samples, lax.all_gather(a_half, 'samp', axis=0, tiled=True), pref...  20.2 us
  transfers between devices with their start and end apart: 8, of which 8 were waited for; matrix products, arithmetic and copies ran while one was open for 4% of the time, Pallas kernels for 0%

commit v1 on v0

v1 whole, which is shorter than its diff:
```python
import jax
import jax.numpy as jnp
from jax import lax
from jax.sharding import PartitionSpec as P

ITERS = 2


step_size = 0.00025


def moment_owned(samples, square):
    partial_moment = lax.dot_general(
        samples, square, (((0,), (0,)), ((), ())), preferred_element_type=jnp.float32
    )
    return lax.psum_scatter(
        partial_moment.astype(jnp.bfloat16), "samp", scatter_dimension=0, tiled=True
    ).astype(jnp.float32)


def model_term(rows, gram):
    return jnp.dot(
        rows, gram * gram, precision=lax.Precision.HIGHEST, preferred_element_type=jnp.float32
    )


def local(samples, factor):
    count = samples.shape[0]
    total = count * lax.axis_size("samp")
    inv_root = 1.0 / jnp.sqrt(jnp.float32(total))
    current = factor
    gradient = jnp.zeros_like(factor)
    for step in range(ITERS):
        block = lax.all_gather(current.astype(jnp.bfloat16), "samp", axis=0, tiled=True)
        proj = jnp.dot(samples, block, preferred_element_type=jnp.float32)
        gram = lax.dot_general(
            block, block, (((0,), (0,)), ((), ())), preferred_element_type=jnp.float32
        )
        both = lax.psum(jnp.concatenate([proj, gram], axis=0), "feat")
        proj, gram = both[:count], both[count:]
        square = (proj * proj).astype(jnp.bfloat16)
        moment = moment_owned(samples, square)
        gradient = moment * inv_root - model_term(current, gram)
        current = current + step_size * gradient
    return (current, gradient)


def solution(mesh):
    in_specs = (P("samp", "feat"), P(("feat", "samp"), None))
    out_specs = (P(("feat", "samp"), None), P(("feat", "samp"), None))
    return jax.shard_map(local, mesh=mesh, in_specs=in_specs, out_specs=out_specs, check_vma=False)
```

time: 657 us -> 361 us (0.55)
  waiting for transfers between devices: 590 us -> 292 us
    psum x4 -> x2, waiting for transfers between devices: 265 us -> 43.4 us  [local(): both = lax.psum(jnp.concatenate([proj, gram], axis=0), 'feat')]
    reduce_scatter x2, waiting for transfers between devices: 219 us -> 144 us  [moment_owned(): lax.psum_scatter(partial_moment.astype(jnp.bfloat16), 'samp', scatter_dim...]
  transfers between devices with their start and end apart: 8 -> 6, of which waited for: 8 -> 6; matrix products, arithmetic and copies ran while one was open for 4% -> 0% of each run, Pallas kernels for 0% -> 0%
where the time goes in v1:
time: 361 us
  waiting for transfers between devices  292 us (81%)
  matrix products  45.8 us (13%)
  between operations  14.2 us (4%)
  local copies, waits for them, and re-layouts  5.29 us (1%)
    reduce_scatter x2, waiting for transfers between devices, moment_owned(): lax.psum_scatter(partial_moment.astype(jnp.bfloat16), 'samp', scatter_dim...  144 us
    all_gather x2, waiting for transfers between devices, local(): lax.all_gather(current.astype(jnp.bfloat16), 'samp', axis=0, tiled=True)  105 us
    psum x2, waiting for transfers between devices, local(): both = lax.psum(jnp.concatenate([proj, gram], axis=0), 'feat')  43.4 us
    dot_general x2, matrix products, moment_owned(): lax.dot_general(samples, square, (((0,), (0,)), ((), ())), preferred_elem...  18 us
    dot_general x2, matrix products, local(): proj = jnp.dot(samples, block, preferred_element_type=jnp.float32)  14 us
    dot_general x2, matrix products, local(): lax.dot_general(block, block, (((0,), (0,)), ((), ())), preferred_element...  9.73 us
  transfers between devices with their start and end apart: 6, of which 6 were waited for; matrix products, arithmetic and copies ran while one was open for 0% of the time, Pallas kernels for 0%

profile of v1, /device:TPU:0, one launch (start us, length us, event | category | flops | bytes accessed | tf_op | source)
XLA Modules:
  0.0 361.0 jit_solution(4212628078614325365)
XLA Ops:
  7.2 0.0 all-gather.3.cloned.1.call-start
  7.2 1.8 convert_element_type.30
  9.0 0.0 all-gather.3.cloned.1.call-update
  9.0 0.0 all-reduce.3.cloned.1.call-start
  9.1 55.0 %all-gather.3.cloned.1.call-done = bf16[16384,128]{1,0:T(8,128)(2,1)} async-done(((bf16[1024,128]{1,0:T(8,128)(2,1)}), bf16[16384,128]{1,0:T(8,128)(2,1)}) %all-gather.3.cloned.1.call-update) | async-done | bytes 4194320 | tf_op jit(solution)/shard_map/all_gather | solution.py:34
  64.0 0.0 copy-start
  64.0 4.9 %fusion.11 = f32[128,128]{1,0:T(8,128)S(1)} fusion(bf16[16384,128]{1,0:T(8,128)(2,1)} %all-gather.3.cloned.1.call-done), kind=kOutput, calls=%fused_computation.21 | convolution fusion | flops 536870912 | bytes 4259840 | tf_op jit(solution)/shard_map/dot_general | solution.py:36
  68.9 2.1 copy-done
  71.1 5.6 %fusion.10 = f32[384,128]{1,0:T(8,128)S(1)} fusion(bf16[384,16384]{1,0:T(8,128)(2,1)S(1)} %copy-done, bf16[16384,128]{1,0:T(8,128)(2,1)} %all-gather.3.cloned.1.call-done), kind=kOutput, calls=%fused_computation.20 | convolution fusion | flops 1610612736 | bytes 16973824 | tf_op jit(solution)/shard_map/dot_general | solution.py:35
  76.7 0.7 pad_maximum_fusion
  77.4 0.0 all-reduce.3.cloned.1.call-update
  77.4 0.0 reduce-scatter.3.cloned.1.call-start
  77.5 21.8 %all-reduce.3.cloned.1.call-done = f32[512,128]{1,0:T(8,128)} async-done(((f32[512,128]{1,0:T(8,128)}), f32[512,128]{1,0:T(8,128)}) %all-reduce.3.cloned.1.call-update) | async-done | bytes 262160 | tf_op jit(solution)/shard_map/psum | solution.py:39
  99.3 9.0 %fusion = bf16[16384,128]{0,1:T(8,128)(2,1)} fusion(bf16[384,16384]{1,0:T(8,128)(2,1)} %param.2, f32[512,128]{1,0:T(8,128)} %all-reduce.3.cloned.1.call-done), kind=kOutput, calls=%fused_computation.2 | convolution fusion | flops 1612808192 | bytes 16973824 | tf_op jit(solution)/shard_map/dot_general | solution.py:13
  108.3 0.0 copy-start.2
  108.3 0.0 reduce-scatter.3.cloned.1.call-update
  108.3 0.0 all-gather.5.cloned.1.call-start
  108.4 1.0 copy-done.2
  109.3 0.2 copy.4
  109.5 71.3 %reduce-scatter.3.cloned.1.call-done = bf16[1024,128]{0,1:T(8,128)(2,1)} async-done(((bf16[16384,128]{0,1:T(8,128)(2,1)}), bf16[1024,128]{0,1:T(8,128)(2,1)}) %reduce-scatter.3.cloned.1.call-update) | async-done | bytes 262160 | tf_op jit(solution)/shard_map/reduce_scatter | solution.py:16
  180.8 2.4 fusion.9
  183.3 0.0 all-gather.5.cloned.1.call-update
  183.3 0.0 all-reduce.5.cloned.1.call-start
  183.3 49.8 %all-gather.5.cloned.1.call-done = bf16[16384,128]{0,1:T(8,128)(2,1)} async-done(((bf16[1024,128]{0,1:T(8,128)(2,1)}), bf16[16384,128]{0,1:T(8,128)(2,1)}) %all-gather.5.cloned.1.call-update) | async-done | bytes 4194320 | tf_op jit(solution)/shard_map/all_gather | solution.py:34
  233.2 0.0 copy-start.1
  233.2 4.8 %fusion.12 = f32[128,128]{0,1:T(8,128)S(1)} fusion(bf16[16384,128]{0,1:T(8,128)(2,1)} %all-gather.5.cloned.1.call-done), kind=kOutput, calls=%fused_computation.22 | convolution fusion | flops 536870912 | bytes 4259840 | tf_op jit(solution)/shard_map/dot_general | solution.py:36
  238.0 0.0 copy-done.1
  238.0 8.4 %convolution_bitcast_fusion.1 = f32[384,128]{0,1:T(8,128)S(1)} fusion(bf16[16384,128]{0,1:T(8,128)(2,1)S(1)} %copy-done.1, bf16[384,16384]{1,0:T(8,128)(2,1)} %param.2), kind=kOutput, calls=%fused_computation.9 | convolution fusion | flops 1610612736 | bytes 16973824 | tf_op jit(solution)/shard_map/dot_general | solution.py:35
  246.4 0.7 pad_maximum_fusion.1
  247.1 0.0 all-reduce.5.cloned.1.call-update
  247.2 0.2 reduce-scatter.5.cloned.1.call-start
  247.4 21.6 %all-reduce.5.cloned.1.call-done = f32[512,128]{0,1:T(8,128)} async-done(((f32[512,128]{0,1:T(8,128)}), f32[512,128]{0,1:T(8,128)}) %all-reduce.5.cloned.1.call-update) | async-done | bytes 262160 | tf_op jit(solution)/shard_map/psum | solution.py:39
  269.0 9.0 %fusion.1 = bf16[16384,128]{0,1:T(8,128)(2,1)} fusion(bf16[384,16384]{1,0:T(8,128)(2,1)} %param.2, f32[512,128]{0,1:T(8,128)} %all-reduce.5.cloned.1.call-done), kind=kOutput, calls=%fused_computation.3 | convolution fusion | flops 1612808192 | bytes 16973824 | tf_op jit(solution)/shard_map/dot_general | solution.py:13
  278.0 0.0 reduce-scatter.5.cloned.1.call-update
  278.0 72.5 %reduce-scatter.5.cloned.1.call-done = bf16[1024,128]{0,1:T(8,128)(2,1)} async-done(((bf16[16384,128]{0,1:T(8,128)(2,1)}), bf16[1024,128]{0,1:T(8,128)(2,1)}) %reduce-scatter.5.cloned.1.call-update) | async-done | bytes 262160 | tf_op jit(solution)/shard_map/reduce_scatter | solution.py:16
  350.5 1.6 multiply_add_fusion
  352.2 1.0 copy.7
  353.2 1.0 copy.8
Async XLA Ops:
  7.2 56.9 %all-gather.3.cloned.1.call-start = ((), (), s32[]{:S(2)}) async-start(), calls=%async_computation.2 | async-start | bytes 4456448 | tf_op jit(solution)/shard_map/all_gather | solution.py:34
  9.0 90.3 %all-reduce.3.cloned.1.call-start = ((), (), s32[]{:S(2)}) async-start(), calls=%async_computation.3 | async-start | bytes 524288 | tf_op jit(solution)/shard_map/psum | solution.py:39
  64.0 7.0 %copy-start = (bf16[384,16384]{1,0:T(8,128)(2,1)S(1)}, bf16[384,16384]{1,0:T(8,128)(2,1)}, u32[]{:S(2)}) copy-start(bf16[384,16384]{1,0:T(8,128)(2,1)} %param.2) | copy-start | bytes 37748740
  77.4 103.4 %reduce-scatter.3.cloned.1.call-start = ((), (), s32[]{:S(2)}) async-start(), calls=%async_computation.4 | async-start | bytes 4456448 | tf_op jit(solution)/shard_map/reduce_scatter | solution.py:16
  108.3 1.0 copy-start.2
  108.3 124.8 %all-gather.5.cloned.1.call-start = ((), (), s32[]{:S(2)}) async-start(), calls=%async_computation.5 | async-start | bytes 4456448 | tf_op jit(solution)/shard_map/all_gather | solution.py:34
  183.3 85.7 %all-reduce.5.cloned.1.call-start = ((), (), s32[]{:S(2)}) async-start(), calls=%async_computation.6 | async-start | bytes 524288 | tf_op jit(solution)/shard_map/psum | solution.py:39
  233.2 4.9 %copy-start.1 = (bf16[16384,128]{0,1:T(8,128)(2,1)S(1)}, bf16[16384,128]{0,1:T(8,128)(2,1)}, u32[]{:S(2)}) copy-start(bf16[16384,128]{0,1:T(8,128)(2,1)} %all-gather.5.cloned.1.call-done) | copy-start | bytes 12582916
  247.2 103.4 %reduce-scatter.5.cloned.1.call-start = ((), (), s32[]{:S(2)}) async-start(), calls=%async_computation.7 | async-start | bytes 4456448 | tf_op jit(solution)/shard_map/reduce_scatter | solution.py:16
Sparse Core Ops, SparseCore 0:
  10.7 53.2 all-gather.2
  77.5 21.6 all-reduce.2
  108.4 72.3 reduce-scatter.2
  183.5 49.6 all-gather.4
  247.3 21.6 all-reduce.4
  278.1 72.3 reduce-scatter.4

commit v2 on v1

v2 whole, which is shorter than its diff:
```python
import functools

import jax
import jax.numpy as jnp
from jax import lax
from jax.experimental import pallas as pl
from jax.experimental.pallas import tpu as pltpu
from jax.sharding import PartitionSpec as P

ITERS = 2


step_size = 0.00025

MESH = pl.DeviceIdType.MESH
f32 = jnp.float32
bf16 = jnp.bfloat16


def kernel(
    L, nf, S, B, inv_root,
    samples, factor, out_cur, out_grad,
    sv, G, part, sq, frecv, acc, dbuf, ybuf, zbuf, drecv, yrecv, zrecv, model,
    s_in, g_recv, g_z, g_y, g_d, f_send, f_recv, d_send, d_recv, y_send, y_recv, z_send, z_recv,
):
    R = factor.shape[1]
    f = lax.axis_index("feat")
    s = lax.axis_index("samp")
    c, y, l = s % 2, (s // 2) % 2, s // 4
    below, above = l > 0, l < L - 1
    dev_d = (f, l * 4 + y * 2 + (1 - c))
    dev_y = (f, l * 4 + (1 - y) * 2 + c)
    dev_dn = (f, s - 4)
    dev_up = (f, s + 4)

    def dev_f(k):
        return (lax.rem(f + k, nf), s)

    load = pltpu.make_async_copy(samples, sv, s_in)
    load.start()

    barrier = pltpu.get_barrier_semaphore()

    def greet(dev):
        pl.semaphore_signal(barrier, inc=1, device_id=dev, device_id_type=MESH)

    greet(dev_d)
    greet(dev_y)
    for k in range(1, nf):
        greet(dev_f(k))

    @pl.when(below)
    def _():
        greet(dev_dn)

    @pl.when(above)
    def _():
        greet(dev_up)

    pl.semaphore_wait(barrier, nf + 1 + jnp.where(below, 1, 0) + jnp.where(above, 1, 0))

    def remote(src, dst, ssem, rsem, dev):
        return pltpu.make_async_remote_copy(
            src_ref=src, dst_ref=dst, send_sem=ssem, recv_sem=rsem,
            device_id=dev, device_id_type=MESH,
        )

    def block(p, core):
        return G.at[p, pl.ds(pl.multiple_of(core * B, B), B)]

    def g_copy(p, core, ssem, dev):
        ref = block(p, core)
        return remote(ref, ref, ssem, g_recv.at[p, core], dev)

    def g_to_dn(lb):
        return g_copy(lb * 2 + y, c, g_z.at[0, lb], dev_dn)

    def g_to_up(lb):
        return g_copy(lb * 2 + y, c, g_z.at[1, lb], dev_up)

    def g_to_y(lb):
        return g_copy(lb * 2 + y, c, g_y.at[lb], dev_y)

    def g_to_d(p):
        return g_copy(p, c, g_d.at[p], dev_d)

    def g_wait(p, core):
        g_copy(p, core, g_d.at[p], dev_d).wait_recv()

    def f_copy(it, k, which):
        rows = pl.ds(0, S) if which == 0 else pl.ds(S, R)
        return remote(
            part.at[rows], frecv.at[it, k - 1, rows],
            f_send.at[k - 1, which], f_recv.at[it, k - 1, which], dev_f(k),
        )

    def d_copy(p):
        return remote(dbuf.at[p], drecv.at[p], d_send.at[p], d_recv.at[p], dev_d)

    def y_copy(lb):
        return remote(ybuf.at[lb], yrecv.at[lb], y_send.at[lb], y_recv.at[lb], dev_y)

    def z_copy(way, lb):
        return remote(
            zbuf.at[lb], zrecv.at[way, lb], z_send.at[lb], z_recv.at[way, lb],
            dev_up if way == 0 else dev_dn,
        )

    def columns(p):
        return pl.ds(pl.multiple_of(p * (2 * B), 2 * B), 2 * B)

    def project(p):
        rows = G[p]
        part[0:S, :] += jnp.dot(sv[:, columns(p)], rows, preferred_element_type=f32)
        part[S : S + R, :] += lax.dot_general(
            rows, rows, (((0,), (0,)), ((), ())), preferred_element_type=f32
        )

    def inside(side, d):
        lb = l + side * d
        ok = (lb >= 0) & (lb < L) & (d >= 0)
        if side > 0:
            ok = ok & (d > 0)
        return lb, ok

    out_cur[...] = factor[...]

    def iteration(it, carry):
        G[l * 2 + y, pl.ds(pl.multiple_of(c * B, B), B), :] = out_cur[...].astype(bf16)

        @pl.when(below)
        def _():
            g_to_dn(l).start()

        @pl.when(above)
        def _():
            g_to_up(l).start()

        g_to_y(l).start()
        g_to_d(l * 2 + y).start()
        part[...] = jnp.zeros_like(part)

        @pl.when(it == 0)
        def _():
            load.wait()

        def gather_step(d, carry):
            for side in (-1, 1):
                lb, ok = inside(side, d)

                @pl.when(ok & (d > 0))
                def _():
                    g_wait(lb * 2 + y, c)
                    if side < 0:

                        @pl.when(above)
                        def _():
                            g_to_up(lb).start()
                    else:

                        @pl.when(below)
                        def _():
                            g_to_dn(lb).start()

                    g_to_y(lb).start()
                    g_to_d(lb * 2 + y).start()

            for side in (-1, 1):
                lb, ok = inside(side, d - 1)

                @pl.when(ok)
                def _():
                    g_wait(lb * 2 + 1 - y, c)
                    g_to_d(lb * 2 + 1 - y).start()

            for side in (-1, 1):
                lb, ok = inside(side, d)

                @pl.when(ok)
                def _():
                    g_wait(lb * 2 + y, 1 - c)
                    project(lb * 2 + y)

            for side in (-1, 1):
                lb, ok = inside(side, d - 1)

                @pl.when(ok)
                def _():
                    g_wait(lb * 2 + 1 - y, 1 - c)
                    project(lb * 2 + 1 - y)

            return carry

        lax.fori_loop(0, L + 1, gather_step, 0)

        for which in (0, 1):
            for k in range(1, nf):
                f_copy(it, k, which).start()

        def gather_sent(lb, carry):
            @pl.when((lb <= l) & above)
            def _():
                g_to_up(lb).wait_send()

            @pl.when((lb >= l) & below)
            def _():
                g_to_dn(lb).wait_send()

            g_to_y(lb).wait_send()
            g_to_d(lb * 2).wait_send()
            g_to_d(lb * 2 + 1).wait_send()
            return carry

        lax.fori_loop(0, L, gather_sent, 0)

        proj = part[0:S, :]
        for k in range(1, nf):
            f_copy(it, k, 0).wait_recv()
            proj = proj + frecv[it, k - 1, 0:S, :]
        sq[...] = (proj * proj).astype(bf16)

        def moment(p):
            m = lax.dot_general(
                sv[:, columns(p)], sq[...], (((0,), (0,)), ((), ())),
                preferred_element_type=f32,
            )
            lo, hi = m[:B], m[B:]
            acc[p] = jnp.where(c == 0, lo, hi)
            dbuf[p] = jnp.where(c == 0, hi, lo).astype(bf16)
            d_copy(p).start()

        def moment_step(i, carry):
            d = L - 1 - i
            for side in (-1, 1):
                lb, ok = inside(side, d)

                @pl.when(ok)
                def _():
                    p = lb * 2 + 1 - y
                    moment(p)
                    moment(lb * 2 + y)
                    d_copy(p).wait_recv()
                    ybuf[lb] = (acc[p] + drecv[p].astype(f32)).astype(bf16)
                    y_copy(lb).start()

            return carry

        lax.fori_loop(0, L, moment_step, 0)

        gram = part[S : S + R, :]
        for k in range(1, nf):
            f_copy(it, k, 1).wait_recv()
            gram = gram + frecv[it, k - 1, S : S + R, :]
        model[...] = jnp.dot(
            out_cur[...], gram * gram, precision=lax.Precision.HIGHEST,
            preferred_element_type=f32,
        )

        def line_step(i, carry):
            d = L - 1 - i
            for side in (-1, 1):
                lb, ok = inside(side, d)

                @pl.when(ok & (d > 0))
                def _():
                    p = lb * 2 + y
                    d_copy(p).wait_recv()
                    y_copy(lb).wait_recv()
                    way = 0 if side > 0 else 1
                    acc[p] = acc[p] + drecv[p].astype(f32) + yrecv[lb].astype(f32)

                    @pl.when(below if side > 0 else above)
                    def _():
                        z_copy(way, lb).wait_recv()
                        acc[p] = acc[p] + zrecv[way, lb].astype(f32)

                    zbuf[lb] = acc[p].astype(bf16)
                    z_copy(way, lb).start()

            return carry

        lax.fori_loop(0, L - 1, line_step, 0)

        own = l * 2 + y
        d_copy(own).wait_recv()
        y_copy(l).wait_recv()
        acc[own] = acc[own] + drecv[own].astype(f32) + yrecv[l].astype(f32)

        @pl.when(below)
        def _():
            z_copy(0, l).wait_recv()
            acc[own] = acc[own] + zrecv[0, l].astype(f32)

        @pl.when(above)
        def _():
            z_copy(1, l).wait_recv()
            acc[own] = acc[own] + zrecv[1, l].astype(f32)

        gradient = acc[own] * inv_root - model[...]
        out_grad[...] = gradient
        out_cur[...] = out_cur[...] + step_size * gradient

        def moment_sent(lb, carry):
            d_copy(lb * 2).wait_send()
            d_copy(lb * 2 + 1).wait_send()
            y_copy(lb).wait_send()

            @pl.when(lb != l)
            def _():
                z_copy(0, lb).wait_send()

            return carry

        lax.fori_loop(0, L, moment_sent, 0)
        for k in range(1, nf):
            for which in (0, 1):
                f_copy(it, k, which).wait_send()
        return carry

    lax.fori_loop(0, ITERS, iteration, 0)


def solution(mesh):
    nf, ns = mesh.shape["feat"], mesh.shape["samp"]
    L = ns // 4

    def local(samples, factor):
        S, W = samples.shape
        B, R = factor.shape
        inv_root = 1.0 / float(S * ns) ** 0.5
        DMA = pltpu.SemaphoreType.DMA
        V = pltpu.VMEM
        scratch = [
            V((S, W), bf16),
            V((2 * L, 2 * B, R), bf16),
            V((S + R, R), f32),
            V((S, R), bf16),
            V((ITERS, max(nf - 1, 1), S + R, R), f32),
            V((2 * L, B, R), f32),
            V((2 * L, B, R), bf16),
            V((L, B, R), bf16),
            V((L, B, R), bf16),
            V((2 * L, B, R), bf16),
            V((L, B, R), bf16),
            V((2, L, B, R), bf16),
            V((B, R), f32),
            DMA,
            DMA((2 * L, 2)),
            DMA((2, L)),
            DMA((L,)),
            DMA((2 * L,)),
            DMA((max(nf - 1, 1), 2)),
            DMA((ITERS, max(nf - 1, 1), 2)),
            DMA((2 * L,)),
            DMA((2 * L,)),
            DMA((L,)),
            DMA((L,)),
            DMA((L,)),
            DMA((2, L)),
        ]
        flops = ITERS * 4 * S * W * R
        return pl.pallas_call(
            functools.partial(kernel, L, nf, S, B, inv_root),
            out_shape=(
                jax.ShapeDtypeStruct((B, R), f32),
                jax.ShapeDtypeStruct((B, R), f32),
            ),
            in_specs=[
                pl.BlockSpec(memory_space=pl.ANY),
                pl.BlockSpec(memory_space=pltpu.VMEM),
            ],
            out_specs=(
                pl.BlockSpec(memory_space=pltpu.VMEM),
                pl.BlockSpec(memory_space=pltpu.VMEM),
            ),
            scratch_shapes=scratch,
            compiler_params=pltpu.CompilerParams(
                collective_id=0, has_side_effects=True, vmem_limit_bytes=56 * 2**20
            ),
            cost_estimate=pl.CostEstimate(
                flops=flops, bytes_accessed=2 * S * W, transcendentals=0
            ),
        )(samples, factor)

    in_specs = (P("samp", "feat"), P(("feat", "samp"), None))
    out_specs = (P(("feat", "samp"), None), P(("feat", "samp"), None))
    return jax.shard_map(local, mesh=mesh, in_specs=in_specs, out_specs=out_specs, check_vma=False)
```

time: 361 us -> 138 us (0.38)
  the two profiles are of different devices: /device:TPU:0 before, /device:TPU:6 now
where the time goes in v2:
time: 138 us; the launch traced here: 137 us
  Pallas kernels  133 us (96%)
  local copies, waits for them, and re-layouts  3.74 us (3%)
    pallas_call x1, Pallas kernels, local(): pl.pallas_call(functools.partial(kernel, L, nf, S, B, inv_root), out_shap...  133 us
    unnamed x2, local copies, waits for them, and re-layouts  3.74 us

profile of v2, /device:TPU:6, one launch (start us, length us, event | category | flops | bytes accessed | tf_op | source)
XLA Modules:
  0.0 137.5 jit_solution(4290126869058870166)
XLA Ops:
  0.6 133.1 %shard_map.41 = (f32[1024,128]{1,0:T(8,128)}, f32[1024,128]{1,0:T(8,128)}) custom-call(bf16[384,16384]{1,0:T(8,128)(2,1)} %samples.1, f32[1024,128]{1,0:T(8,128)} %factor.1), custom_call_target="tpu_custom_call" | custom-call | flops 6442450944 | bytes 12582912 | tf_op jit(solution)/shard_map/pallas_call | solution.py:362
  133.7 1.9 %copy.6 = f32[1024,128]{1,0:T(8,128)} copy(f32[1024,128]{1,0:T(8,128)} %get-tuple-element.4) | data formatting | bytes 1048576
  135.6 1.9 %copy.7 = f32[1024,128]{1,0:T(8,128)} copy(f32[1024,128]{1,0:T(8,128)} %get-tuple-element.5) | data formatting | bytes 1048576

commit v3 on v2

v3 whole, which is shorter than its diff:
```python
import functools

import jax
import jax.numpy as jnp
from jax import lax
from jax.experimental import pallas as pl
from jax.experimental.pallas import tpu as pltpu
from jax.sharding import PartitionSpec as P

ITERS = 2


step_size = 0.00025

MESH = pl.DeviceIdType.MESH
f32 = jnp.float32
bf16 = jnp.bfloat16


def kernel(
    L, nf, S, B, inv_root,
    samples, factor, out_cur, out_grad,
    sv, G, part, rest, rest_half, sq, frecv, frecv_half, frecv_gram, acc, dbuf, ybuf, zbuf, drecv, yrecv, zrecv, model,
    s_in, g_recv, g_z, g_y, g_d, f_send, f_recv, d_send, d_recv, y_send, y_recv, z_send, z_recv,
):
    R = factor.shape[1]
    f = lax.axis_index("feat")
    s = lax.axis_index("samp")
    c, y, l = s % 2, (s // 2) % 2, s // 4
    below, above = l > 0, l < L - 1
    dev_d = (f, l * 4 + y * 2 + (1 - c))
    dev_y = (f, l * 4 + (1 - y) * 2 + c)
    dev_dn = (f, s - 4)
    dev_up = (f, s + 4)

    def dev_f(k):
        return (lax.rem(f + k, nf), s)

    load = pltpu.make_async_copy(samples, sv, s_in)
    load.start()

    barrier = pltpu.get_barrier_semaphore()

    def greet(dev):
        pl.semaphore_signal(barrier, inc=1, device_id=dev, device_id_type=MESH)

    greet(dev_d)
    greet(dev_y)
    for k in range(1, nf):
        greet(dev_f(k))

    @pl.when(below)
    def _():
        greet(dev_dn)

    @pl.when(above)
    def _():
        greet(dev_up)

    pl.semaphore_wait(barrier, nf + 1 + jnp.where(below, 1, 0) + jnp.where(above, 1, 0))

    def remote(src, dst, ssem, rsem, dev):
        return pltpu.make_async_remote_copy(
            src_ref=src, dst_ref=dst, send_sem=ssem, recv_sem=rsem,
            device_id=dev, device_id_type=MESH,
        )

    Bh = B // 2
    halves = (0, 1)

    def half(h):
        return pl.ds(h * Bh, Bh)

    def g_copy(p, core, h, ssem, dev):
        ref = G.at[p, pl.ds(pl.multiple_of(core * B + h * Bh, Bh), Bh)]
        return remote(ref, ref, ssem, g_recv.at[p, core, h], dev)

    def g_to_dn(lb, h):
        return g_copy(lb * 2 + y, c, h, g_z.at[0, lb, h], dev_dn)

    def g_to_up(lb, h):
        return g_copy(lb * 2 + y, c, h, g_z.at[1, lb, h], dev_up)

    def g_to_y(lb, h):
        return g_copy(lb * 2 + y, c, h, g_y.at[lb, h], dev_y)

    def g_to_d(p, h):
        return g_copy(p, c, h, g_d.at[p, h], dev_d)

    def g_wait(p, core, h):
        g_copy(p, core, h, g_d.at[p, h], dev_d).wait_recv()

    def f_copy(it, k, which):
        src, dst = (
            (part, frecv), (rest_half, frecv_half), (rest.at[pl.ds(S, R)], frecv_gram)
        )[which]
        return remote(
            src, dst.at[it, k - 1],
            f_send.at[k - 1, which], f_recv.at[it, k - 1, which], dev_f(k),
        )

    def d_copy(p):
        return remote(dbuf.at[p], drecv.at[p], d_send.at[p], d_recv.at[p], dev_d)

    def y_copy(lb, h):
        return remote(
            ybuf.at[lb, half(h)], yrecv.at[lb, half(h)], y_send.at[lb, h], y_recv.at[lb, h], dev_y
        )

    def z_copy(way, lb, h):
        return remote(
            zbuf.at[lb, half(h)], zrecv.at[way, lb, half(h)],
            z_send.at[lb, h], z_recv.at[way, lb, h],
            dev_up if way == 0 else dev_dn,
        )

    def columns(p):
        return pl.ds(pl.multiple_of(p * (2 * B), 2 * B), 2 * B)

    def project(p, into):
        rows = G[p]
        into[0:S, :] += jnp.dot(sv[:, columns(p)], rows, preferred_element_type=f32)
        into[S : S + R, :] += lax.dot_general(
            rows, rows, (((0,), (0,)), ((), ())), preferred_element_type=f32
        )

    def inside(side, d):
        lb = l + side * d
        ok = (lb >= 0) & (lb < L) & (d >= 0)
        if side > 0:
            ok = ok & (d > 0)
        return lb, ok

    out_cur[...] = factor[...]

    def iteration(it, carry):
        G[l * 2 + y, pl.ds(pl.multiple_of(c * B, B), B), :] = out_cur[...].astype(bf16)

        for h in halves:

            @pl.when(below)
            def _():
                g_to_dn(l, h).start()

            @pl.when(above)
            def _():
                g_to_up(l, h).start()

            g_to_y(l, h).start()
            g_to_d(l * 2 + y, h).start()
        part[...] = jnp.zeros_like(part)
        rest[...] = jnp.zeros_like(rest)

        @pl.when(it == 0)
        def _():
            load.wait()

        def gather_step(d, into):
            for side in (-1, 1):
                lb, ok = inside(side, d)

                @pl.when(ok & (d > 0))
                def _():
                    for h in halves:
                        g_wait(lb * 2 + y, c, h)
                        if side < 0:

                            @pl.when(above)
                            def _():
                                g_to_up(lb, h).start()
                        else:

                            @pl.when(below)
                            def _():
                                g_to_dn(lb, h).start()

                        g_to_y(lb, h).start()
                        g_to_d(lb * 2 + y, h).start()

            for side in (-1, 1):
                lb, ok = inside(side, d - 1)

                @pl.when(ok)
                def _():
                    for h in halves:
                        g_wait(lb * 2 + 1 - y, c, h)
                        g_to_d(lb * 2 + 1 - y, h).start()

            for side in (-1, 1):
                lb, ok = inside(side, d)

                @pl.when(ok)
                def _():
                    for h in halves:
                        g_wait(lb * 2 + y, 1 - c, h)
                    project(lb * 2 + y, into)

            for side in (-1, 1):
                lb, ok = inside(side, d - 1)

                @pl.when(ok)
                def _():
                    for h in halves:
                        g_wait(lb * 2 + 1 - y, 1 - c, h)
                    project(lb * 2 + 1 - y, into)

        last = jnp.maximum(l, L - 1 - l) + 1

        def early_step(d, carry):
            gather_step(d, part)
            return carry

        lax.fori_loop(0, last, early_step, 0)
        for k in range(1, nf):
            f_copy(it, k, 0).start()
        gather_step(last, rest)
        rest_half[...] = rest[0:S, :].astype(bf16)
        for k in range(1, nf):
            f_copy(it, k, 1).start()
        for k in range(1, nf):
            f_copy(it, k, 2).start()

        def gather_sent(lb, carry):
            for h in halves:

                @pl.when((lb <= l) & above)
                def _():
                    g_to_up(lb, h).wait_send()

                @pl.when((lb >= l) & below)
                def _():
                    g_to_dn(lb, h).wait_send()

                g_to_y(lb, h).wait_send()
                g_to_d(lb * 2, h).wait_send()
                g_to_d(lb * 2 + 1, h).wait_send()
            return carry

        lax.fori_loop(0, L, gather_sent, 0)

        proj = part[0:S, :] + rest[0:S, :]
        for k in range(1, nf):
            f_copy(it, k, 0).wait_recv()
            f_copy(it, k, 1).wait_recv()
            proj = proj + (frecv[it, k - 1, 0:S, :] + frecv_half[it, k - 1].astype(f32))
        sq[...] = (proj * proj).astype(bf16)

        def moment(p):
            m = lax.dot_general(
                sv[:, columns(p)], sq[...], (((0,), (0,)), ((), ())),
                preferred_element_type=f32,
            )
            lo, hi = m[:B], m[B:]
            acc[p] = jnp.where(c == 0, lo, hi)
            dbuf[p] = jnp.where(c == 0, hi, lo).astype(bf16)
            d_copy(p).start()

        def moment_step(i, carry):
            d = L - 1 - i
            for side in (-1, 1):
                lb, ok = inside(side, d)

                @pl.when(ok)
                def _():
                    p = lb * 2 + 1 - y
                    moment(p)
                    moment(lb * 2 + y)
                    d_copy(p).wait_recv()
                    for h in halves:
                        own = acc[p, half(h)] + drecv[p, half(h)].astype(f32)
                        ybuf[lb, half(h)] = own.astype(bf16)
                        y_copy(lb, h).start()

            return carry

        lax.fori_loop(0, L, moment_step, 0)

        gram = part[S : S + R, :] + rest[S : S + R, :]
        for k in range(1, nf):
            f_copy(it, k, 2).wait_recv()
            gram = gram + (frecv[it, k - 1, S : S + R, :] + frecv_gram[it, k - 1])
        model[...] = jnp.dot(
            out_cur[...], gram * gram, precision=lax.Precision.HIGHEST,
            preferred_element_type=f32,
        )

        def line_step(i, carry):
            d = L - 1 - i
            for side in (-1, 1):
                lb, ok = inside(side, d)

                @pl.when(ok & (d > 0))
                def _():
                    p = lb * 2 + y
                    d_copy(p).wait_recv()
                    way = 0 if side > 0 else 1
                    for h in halves:
                        y_copy(lb, h).wait_recv()
                        acc[p, half(h)] = (
                            acc[p, half(h)] + drecv[p, half(h)].astype(f32)
                            + yrecv[lb, half(h)].astype(f32)
                        )

                        @pl.when(below if side > 0 else above)
                        def _():
                            z_copy(way, lb, h).wait_recv()
                            acc[p, half(h)] = acc[p, half(h)] + zrecv[way, lb, half(h)].astype(f32)

                        zbuf[lb, half(h)] = acc[p, half(h)].astype(bf16)
                        z_copy(way, lb, h).start()

            return carry

        lax.fori_loop(0, L - 1, line_step, 0)

        own = l * 2 + y
        d_copy(own).wait_recv()
        for h in halves:
            y_copy(l, h).wait_recv()
        acc[own] = acc[own] + drecv[own].astype(f32) + yrecv[l].astype(f32)

        @pl.when(below)
        def _():
            for h in halves:
                z_copy(0, l, h).wait_recv()
            acc[own] = acc[own] + zrecv[0, l].astype(f32)

        @pl.when(above)
        def _():
            for h in halves:
                z_copy(1, l, h).wait_recv()
            acc[own] = acc[own] + zrecv[1, l].astype(f32)

        @pl.when(it < ITERS - 1)
        def _():
            gradient = acc[own] * inv_root - model[...]
            out_cur[...] = out_cur[...] + step_size * gradient

        @pl.when(it == ITERS - 1)
        def _():
            out_grad[...] = acc[own] - model[...] * (1.0 / inv_root)

        def moment_sent(lb, carry):
            d_copy(lb * 2).wait_send()
            d_copy(lb * 2 + 1).wait_send()
            for h in halves:
                y_copy(lb, h).wait_send()

            @pl.when(lb != l)
            def _():
                for h in halves:
                    z_copy(0, lb, h).wait_send()

            return carry

        lax.fori_loop(0, L, moment_sent, 0)
        for k in range(1, nf):
            for which in (0, 1, 2):
                f_copy(it, k, which).wait_send()
        return carry

    lax.fori_loop(0, ITERS, iteration, 0)


def solution(mesh):
    nf, ns = mesh.shape["feat"], mesh.shape["samp"]
    L = ns // 4

    def local(samples, factor):
        S, W = samples.shape
        B, R = factor.shape
        inv_root = 1.0 / float(S * ns) ** 0.5
        DMA = pltpu.SemaphoreType.DMA
        V = pltpu.VMEM
        peers = max(nf - 1, 1)
        scratch = [
            V((S, W), bf16),
            V((2 * L, 2 * B, R), bf16),
            V((S + R, R), f32),
            V((S + R, R), f32),
            V((S, R), bf16),
            V((S, R), bf16),
            V((ITERS, peers, S + R, R), f32),
            V((ITERS, peers, S, R), bf16),
            V((ITERS, peers, R, R), f32),
            V((2 * L, B, R), f32),
            V((2 * L, B, R), bf16),
            V((L, B, R), bf16),
            V((L, B, R), bf16),
            V((2 * L, B, R), bf16),
            V((L, B, R), bf16),
            V((2, L, B, R), bf16),
            V((B, R), f32),
            DMA,
            DMA((2 * L, 2, 2)),
            DMA((2, L, 2)),
            DMA((L, 2)),
            DMA((2 * L, 2)),
            DMA((peers, 3)),
            DMA((ITERS, peers, 3)),
            DMA((2 * L,)),
            DMA((2 * L,)),
            DMA((L, 2)),
            DMA((L, 2)),
            DMA((L, 2)),
            DMA((2, L, 2)),
        ]
        flops = ITERS * 4 * S * W * R
        previous, scaled = pl.pallas_call(
            functools.partial(kernel, L, nf, S, B, inv_root),
            out_shape=(
                jax.ShapeDtypeStruct((B, R), f32),
                jax.ShapeDtypeStruct((B, R), f32),
            ),
            in_specs=[
                pl.BlockSpec(memory_space=pl.ANY),
                pl.BlockSpec(memory_space=pltpu.VMEM),
            ],
            out_specs=(
                pl.BlockSpec(memory_space=pltpu.VMEM),
                pl.BlockSpec(memory_space=pltpu.VMEM),
            ),
            scratch_shapes=scratch,
            compiler_params=pltpu.CompilerParams(
                collective_id=0, has_side_effects=True, vmem_limit_bytes=56 * 2**20
            ),
            cost_estimate=pl.CostEstimate(
                flops=flops, bytes_accessed=2 * S * W, transcendentals=0
            ),
        )(samples, factor)
        gradient = scaled * inv_root
        return (previous + step_size * gradient, gradient)

    in_specs = (P("samp", "feat"), P(("feat", "samp"), None))
    out_specs = (P(("feat", "samp"), None), P(("feat", "samp"), None))
    return jax.shard_map(local, mesh=mesh, in_specs=in_specs, out_specs=out_specs, check_vma=False)
```

time: 138 us -> 127 us (0.920)
  the two profiles are of different devices: /device:TPU:6 before, /device:TPU:0 now
where the time goes in v3:
time: 127 us
  Pallas kernels  124 us (98%)
  other arithmetic  2.26 us (2%)
    pallas_call x1, Pallas kernels, local(): pl.pallas_call(functools.partial(kernel, L, nf, S, B, inv_root), out_shap...  124 us

profile of v3, /device:TPU:0, one launch (start us, length us, event | category | flops | bytes accessed | tf_op | source)
XLA Modules:
  0.0 127.1 jit_solution(1244287175863558969)
XLA Ops:
  0.6 124.3 %shard_map.41 = (f32[1024,128]{1,0:T(8,128)}, f32[1024,128]{1,0:T(8,128)}) custom-call(bf16[384,16384]{1,0:T(8,128)(2,1)} %samples.1, f32[1024,128]{1,0:T(8,128)} %factor.1), custom_call_target="tpu_custom_call" | custom-call | flops 6442450944 | bytes 12582912 | tf_op jit(solution)/shard_map/pallas_call | solution.py:409
  124.9 2.3 %broadcast_multiply_fusion = (f32[1024,128]{1,0:T(8,128)}, f32[1024,128]{1,0:T(8,128)}) fusion(f32[1024,128]{1,0:T(8,128)} %get-tuple-element.5, f32[1024,128]{1,0:T(8,128)} %get-tuple-element.4), kind=kLoop, calls=%fused_computation.1 | loop fusion | flops 393216 | bytes 2097152 | tf_op jit(solution)/shard_map/mul | solution.py:431

commit v4 on v3

--- a/solution.py
+++ b/solution.py
@@ -22,6 +22,7 @@
     samples, factor, out_cur, out_grad,
     sv, G, part, rest, rest_half, sq, frecv, frecv_half, frecv_gram, acc, dbuf, ybuf, zbuf, drecv, yrecv, zrecv, model,
     s_in, g_recv, g_z, g_y, g_d, f_send, f_recv, d_send, d_recv, y_send, y_recv, z_send, z_recv,
+    xbuf, xrecv, x_send, x_recv,
 ):
     R = factor.shape[1]
     f = lax.axis_index("feat")
@@ -30,6 +31,10 @@
     below, above = l > 0, l < L - 1
     dev_d = (f, l * 4 + y * 2 + (1 - c))
     dev_y = (f, l * 4 + (1 - y) * 2 + c)
+    spread = L >= 4 and L % 2 == 0
+    n = l + 1 - 2 * (l % 2) if spread else -1
+    dev_n = (f, n * 4 + y * 2 + c)
+    relay_step = jnp.maximum(jnp.where(l % 2 == 0, l, L - 1 - l), 1)
     dev_dn = (f, s - 4)
     dev_up = (f, s + 4)
 
@@ -86,6 +91,12 @@
 
     def g_to_d(p, h):
         return g_copy(p, c, h, g_d.at[p, h], dev_d)
+
+    def g_relay():
+        return g_copy(l * 2 + 1 - y, c, 1, g_z.at[1 - l % 2, n, 1], dev_n)
+
+    def x_copy():
+        return remote(xbuf, xrecv, x_send, x_recv, dev_n)
 
     def g_wait(p, core, h):
         g_copy(p, core, h, g_d.at[p, h], dev_d).wait_recv()
@@ -155,7 +166,7 @@
         def _():
             load.wait()
 
-        def gather_step(d, into):
+        def gather_step(d, into, final=False):
             for side in (-1, 1):
                 lb, ok = inside(side, d)
 
@@ -174,7 +185,14 @@
                             def _():
                                 g_to_dn(lb, h).start()
 
-                        g_to_y(lb, h).start()
+                        if h == 0:
+                            g_to_y(lb, h).start()
+                        else:
+
+                            @pl.when(lb != n)
+                            def _():
+                                g_to_y(lb, h).start()
+
                         g_to_d(lb * 2 + y, h).start()
 
             for side in (-1, 1):
@@ -182,9 +200,23 @@
 
                 @pl.when(ok)
                 def _():
-                    for h in halves:
-                        g_wait(lb * 2 + 1 - y, c, h)
-                        g_to_d(lb * 2 + 1 - y, h).start()
+                    g_wait(lb * 2 + 1 - y, c, 0)
+                    g_to_d(lb * 2 + 1 - y, 0).start()
+
+                    @pl.when(lb != n)
+                    def _():
+                        g_wait(lb * 2 + 1 - y, c, 1)
+                        g_to_d(lb * 2 + 1 - y, 1).start()
+
+            if spread:
+
+                @pl.when(d == relay_step)
+                def _():
+                    g_relay().start()
+
+                if final:
+                    g_wait(n * 2 + 1 - y, c, 1)
+                    g_to_d(n * 2 + 1 - y, 1).start()
 
             for side in (-1, 1):
                 lb, ok = inside(side, d)
@@ -198,12 +230,17 @@
             for side in (-1, 1):
                 lb, ok = inside(side, d - 1)
 
-                @pl.when(ok)
+                @pl.when(ok & (lb != n))
                 def _():
                     for h in halves:
                         g_wait(lb * 2 + 1 - y, 1 - c, h)
                     project(lb * 2 + 1 - y, into)
 
+            if spread and final:
+                for h in halves:
+                    g_wait(n * 2 + 1 - y, 1 - c, h)
+                project(n * 2 + 1 - y, into)
+
         last = jnp.maximum(l, L - 1 - l) + 1
 
         def early_step(d, carry):
@@ -213,7 +250,7 @@
         lax.fori_loop(0, last, early_step, 0)
         for k in range(1, nf):
             f_copy(it, k, 0).start()
-        gather_step(last, rest)
+        gather_step(last, rest, final=True)
         rest_half[...] = rest[0:S, :].astype(bf16)
         for k in range(1, nf):
             f_copy(it, k, 1).start()
@@ -231,12 +268,17 @@
                 def _():
                     g_to_dn(lb, h).wait_send()
 
-                g_to_y(lb, h).wait_send()
+                @pl.when((lb != n) | (h == 0))
+                def _():
+                    g_to_y(lb, h).wait_send()
+
                 g_to_d(lb * 2, h).wait_send()
                 g_to_d(lb * 2 + 1, h).wait_send()
             return carry
 
         lax.fori_loop(0, L, gather_sent, 0)
+        if spread:
+            g_relay().wait_send()
 
         proj = part[0:S, :] + rest[0:S, :]
         for k in range(1, nf):
@@ -263,16 +305,49 @@
                 @pl.when(ok)
                 def _():
                     p = lb * 2 + 1 - y
-                    moment(p)
+
+                    def half_sum(h):
+                        return acc[p, half(h)] + drecv[p, half(h)].astype(f32)
+
+                    @pl.when(lb != n)
+                    def _():
+                        moment(p)
+
                     moment(lb * 2 + y)
+
+                    @pl.when(lb != n)
+                    def _():
+                        d_copy(p).wait_recv()
+
+                    ybuf[lb, half(0)] = half_sum(0).astype(bf16)
+                    y_copy(lb, 0).start()
+
+                    @pl.when((lb != n) & (lb != l) if spread else lb >= 0)
+                    def _():
+                        ybuf[lb, half(1)] = half_sum(1).astype(bf16)
+                        y_copy(lb, 1).start()
+
+                    if spread and side < 0:
+
+                        @pl.when(lb == l)
+                        def _():
+                            x_copy().wait_recv()
+                            ybuf[lb, half(1)] = (half_sum(1) + xrecv[...].astype(f32)).astype(bf16)
+                            y_copy(lb, 1).start()
+
+            if spread:
+
+                @pl.when(i == 0)
+                def _():
+                    p = n * 2 + 1 - y
                     d_copy(p).wait_recv()
-                    for h in halves:
-                        own = acc[p, half(h)] + drecv[p, half(h)].astype(f32)
-                        ybuf[lb, half(h)] = own.astype(bf16)
-                        y_copy(lb, h).start()
+                    xbuf[...] = (acc[p, half(1)] + drecv[p, half(1)].astype(f32)).astype(bf16)
+                    x_copy().start()
 
             return carry
 
+        if spread:
+            moment(n * 2 + 1 - y)
         lax.fori_loop(0, L, moment_step, 0)
 
         gram = part[S : S + R, :] + rest[S : S + R, :]
@@ -295,11 +370,12 @@
                     d_copy(p).wait_recv()
                     way = 0 if side > 0 else 1
                     for h in halves:
-                        y_copy(lb, h).wait_recv()
-                        acc[p, half(h)] = (
-                            acc[p, half(h)] + drecv[p, half(h)].astype(f32)
-                            + yrecv[lb, half(h)].astype(f32)
-                        )
+                        acc[p, half(h)] = acc[p, half(h)] + drecv[p, half(h)].astype(f32)
+
+                        @pl.when((lb != n) | (h == 0))
+                        def _():
+                            y_copy(lb, h).wait_recv()
+                            acc[p, half(h)] = acc[p, half(h)] + yrecv[lb, half(h)].astype(f32)
 
                         @pl.when(below if side > 0 else above)
                         def _():
@@ -343,8 +419,11 @@
         def moment_sent(lb, carry):
             d_copy(lb * 2).wait_send()
             d_copy(lb * 2 + 1).wait_send()
-            for h in halves:
-                y_copy(lb, h).wait_send()
+            y_copy(lb, 0).wait_send()
+
+            @pl.when(lb != n)
+            def _():
+                y_copy(lb, 1).wait_send()
 
             @pl.when(lb != l)
             def _():
@@ -354,6 +433,8 @@
             return carry
 
         lax.fori_loop(0, L, moment_sent, 0)
+        if spread:
+            x_copy().wait_send()
         for k in range(1, nf):
             for which in (0, 1, 2):
                 f_copy(it, k, which).wait_send()
@@ -404,6 +485,10 @@
             DMA((L, 2)),
             DMA((L, 2)),
             DMA((2, L, 2)),
+            V((B // 2, R), bf16),
+            V((B // 2, R), bf16),
+            DMA,
+            DMA,
         ]
         flops = ITERS * 4 * S * W * R
         previous, scaled = pl.pallas_call(

time: 127 us -> 127 us (level); the launches traced: 127 us -> 126 us
    pallas_call x1, Pallas kernels: 124 us -> 123 us  [local(): pl.pallas_call(functools.partial(kernel, L, nf, S, B, inv_root), out_shap...]
where the time goes in v4:
time: 127 us; the launch traced here: 126 us
  Pallas kernels  123 us (97%)
  other arithmetic  2.26 us (2%)
    pallas_call x1, Pallas kernels, local(): pl.pallas_call(functools.partial(kernel, L, nf, S, B, inv_root), out_shap...  123 us

profile of v4, /device:TPU:0, one launch (start us, length us, event | category | flops | bytes accessed | tf_op | source)
XLA Modules:
  0.0 125.8 jit_solution(8055338543109730523)
XLA Ops:
  0.6 122.9 %shard_map.41 = (f32[1024,128]{1,0:T(8,128)}, f32[1024,128]{1,0:T(8,128)}) custom-call(bf16[384,16384]{1,0:T(8,128)(2,1)} %samples.1, f32[1024,128]{1,0:T(8,128)} %factor.1), custom_call_target="tpu_custom_call" | custom-call | flops 6442450944 | bytes 12582912 | tf_op jit(solution)/shard_map/pallas_call | solution.py:494
  123.6 2.3 %broadcast_multiply_fusion = (f32[1024,128]{1,0:T(8,128)}, f32[1024,128]{1,0:T(8,128)}) fusion(f32[1024,128]{1,0:T(8,128)} %get-tuple-element.5, f32[1024,128]{1,0:T(8,128)} %get-tuple-element.4), kind=kLoop, calls=%fused_computation.1 | loop fusion | flops 393216 | bytes 2097152 | tf_op jit(solution)/shard_map/mul | solution.py:516

commit v5 on v3

--- a/solution.py
+++ b/solution.py
@@ -255,6 +255,33 @@
             dbuf[p] = jnp.where(c == 0, hi, lo).astype(bf16)
             d_copy(p).start()
 
+        def line_step(i, carry):
+            d = L - 1 - i
+            for side in (-1, 1):
+                lb, ok = inside(side, d)
+
+                @pl.when(ok & (d > 0))
+                def _():
+                    p = lb * 2 + y
+                    d_copy(p).wait_recv()
+                    way = 0 if side > 0 else 1
+                    for h in halves:
+                        y_copy(lb, h).wait_recv()
+                        acc[p, half(h)] = (
+                            acc[p, half(h)] + drecv[p, half(h)].astype(f32)
+                            + yrecv[lb, half(h)].astype(f32)
+                        )
+
+                        @pl.when(below if side > 0 else above)
+                        def _():
+                            z_copy(way, lb, h).wait_recv()
+                            acc[p, half(h)] = acc[p, half(h)] + zrecv[way, lb, half(h)].astype(f32)
+
+                        zbuf[lb, half(h)] = acc[p, half(h)].astype(bf16)
+                        z_copy(way, lb, h).start()
+
+            return carry
+
         def moment_step(i, carry):
             d = L - 1 - i
             for side in (-1, 1):
@@ -270,6 +297,10 @@
                         own = acc[p, half(h)] + drecv[p, half(h)].astype(f32)
                         ybuf[lb, half(h)] = own.astype(bf16)
                         y_copy(lb, h).start()
+
+            @pl.when(i > 0)
+            def _():
+                line_step(i - 1, 0)
 
             return carry
 
@@ -283,35 +314,6 @@
             out_cur[...], gram * gram, precision=lax.Precision.HIGHEST,
             preferred_element_type=f32,
         )
-
-        def line_step(i, carry):
-            d = L - 1 - i
-            for side in (-1, 1):
-                lb, ok = inside(side, d)
-
-                @pl.when(ok & (d > 0))
-                def _():
-                    p = lb * 2 + y
-                    d_copy(p).wait_recv()
-                    way = 0 if side > 0 else 1
-                    for h in halves:
-                        y_copy(lb, h).wait_recv()
-                        acc[p, half(h)] = (
-                            acc[p, half(h)] + drecv[p, half(h)].astype(f32)
-                            + yrecv[lb, half(h)].astype(f32)
-                        )
-
-                        @pl.when(below if side > 0 else above)
-                        def _():
-                            z_copy(way, lb, h).wait_recv()
-                            acc[p, half(h)] = acc[p, half(h)] + zrecv[way, lb, half(h)].astype(f32)
-
-                        zbuf[lb, half(h)] = acc[p, half(h)].astype(bf16)
-                        z_copy(way, lb, h).start()
-
-            return carry
-
-        lax.fori_loop(0, L - 1, line_step, 0)
 
         own = l * 2 + y
         d_copy(own).wait_recv()

time: 127 us -> 127 us (level)
  no operation moved by 1% of the time
where the time goes in v5:
time: 127 us
  Pallas kernels  124 us (98%)
  other arithmetic  2.26 us (2%)
    pallas_call x1, Pallas kernels, local(): pl.pallas_call(functools.partial(kernel, L, nf, S, B, inv_root), out_shap...  124 us

profile of v5, /device:TPU:0, one launch (start us, length us, event | category | flops | bytes accessed | tf_op | source)
XLA Modules:
  0.0 126.8 jit_solution(17573497252839625136)
XLA Ops:
  0.6 123.9 %shard_map.41 = (f32[1024,128]{1,0:T(8,128)}, f32[1024,128]{1,0:T(8,128)}) custom-call(bf16[384,16384]{1,0:T(8,128)(2,1)} %samples.1, f32[1024,128]{1,0:T(8,128)} %factor.1), custom_call_target="tpu_custom_call" | custom-call | flops 6442450944 | bytes 12582912 | tf_op jit(solution)/shard_map/pallas_call | solution.py:411
  124.5 2.3 %broadcast_multiply_fusion = (f32[1024,128]{1,0:T(8,128)}, f32[1024,128]{1,0:T(8,128)}) fusion(f32[1024,128]{1,0:T(8,128)} %get-tuple-element.5, f32[1024,128]{1,0:T(8,128)} %get-tuple-element.4), kind=kLoop, calls=%fused_computation.1 | loop fusion | flops 393216 | bytes 2097152 | tf_op jit(solution)/shard_map/mul | solution.py:433
